TPU v7x, 32 devices: a whole 2x2x4 slice. The times are simulated.
32 devices in a mesh: seq: 16 (over z, x, core), mp: 2 (over y).
Axes of the slice: x: 2, y: 2, z: 4, core: 2. Of those that a mesh axis runs over, the one named last changes fastest.
Arguments:
- stream_one: float32 [2048, 1024], P('seq'), may hold values from -6 to 6
- stream_two: float32 [2048, 1024], P('seq'), may hold values from -6 to 6
- cotangent_one: float32 [2048, 1024], P('seq'), may hold values from -6 to 6
- cotangent_two: float32 [2048, 1024], P('seq'), may hold values from -6 to 6
- bucket_numbers: int32 [2, 4, 8, 2048], P(None, None, 'mp'), may hold values from 0 to 31, as said below
- query_weight: bfloat16 [2, 1024, 1024], P(None, None, 'mp'), may hold values from -0.25 to 0.25
- value_weight: bfloat16 [2, 1024, 1024], P(None, None, 'mp'), may hold values from -0.1875 to 0.1875
- mixing_weight: bfloat16 [2, 1024, 1024], P(None, 'mp'), may hold values from -0.75 to 0.75
- mixing_bias: float32 [2, 1024], replicated, may hold values from -3 to 3
- expand_weight: bfloat16 [2, 1024, 4096], P(None, None, 'mp'), may hold values from -0.1875 to 0.1875
- expand_bias: float32 [2, 4096], P(None, 'mp'), may hold values from -3 to 3
- shrink_weight: bfloat16 [2, 4096, 1024], P(None, 'mp'), may hold values from -0.125 to 0.125
- shrink_bias: float32 [2, 1024], replicated, may hold values from -3 to 3
- attention_gain: float32 [2, 1024], replicated, may hold values from 0.1 to 1.9
- attention_shift: float32 [2, 1024], replicated, may hold values from -3 to 3
- forward_gain: float32 [2, 1024], replicated, may hold values from 0.1 to 1.9
- forward_shift: float32 [2, 1024], replicated, may hold values from -3 to 3
Outputs:
- result_one: float32 [2048, 1024], P('seq')
- result_two: float32 [2048, 1024], P('seq')
- gradient_one: float32 [2048, 1024], P('seq')
- gradient_two: float32 [2048, 1024], P('seq')
- weight_query: float32 [2, 1024, 1024], P(None, 'seq', 'mp')
- weight_value: float32 [2, 1024, 1024], P(None, 'seq', 'mp')
- weight_mixing: float32 [2, 1024, 1024], P(None, ('mp', 'seq'))
- bias_mixing: float32 [2, 1024], P(None, 'seq')
- weight_expand: float32 [2, 1024, 4096], P(None, 'seq', 'mp')
- bias_expand: float32 [2, 4096], P(None, ('mp', 'seq'))
- weight_shrink: float32 [2, 4096, 1024], P(None, ('mp', 'seq'))
- bias_shrink: float32 [2, 1024], P(None, 'seq')
- gain_attention: float32 [2, 1024], P(None, 'seq')
- shift_attention: float32 [2, 1024], P(None, 'seq')
- gain_forward: float32 [2, 1024], P(None, 'seq')
- shift_forward: float32 [2, 1024], P(None, 'seq')
Inputs may be any that keep to these rules, and one draw needn't show every extreme that they name: `bucket_numbers`: for every layer, round and head, the tokens whose bucket number lies in bucket numbers p * (2) to (p + 1) * 2 - 1 are exactly 128 for every p, so that sorted rows p * 128 to (p + 1) * 128 - 1 are these tokens; of one block of 128 consecutive positions at most 16 lie in one such range. Buckets hold uneven numbers of tokens.
All inputs are finite; a program needn't handle non-finite values.
Results may differ from a plain program's by a relative error of at most 0.014.
Values may be sent and summed in bfloat16 or wider, within the bound.
A program may use at most 192 MiB of HBM per device.

v0:
```python
import math

import jax
import jax.numpy as jnp
from jax import lax
from jax.sharding import PartitionSpec as P

DH = 128
SPAN = 64
ROUNDS = 4
LAYERS = 2


precise = lax.Precision.HIGHEST


def passed_along(block, axis, distance):
    devices = range(lax.axis_size(axis))
    route = [((i - distance) % len(devices), i) for i in devices]
    return lax.ppermute(block, axis, route)


def layer_norm(values, scale_row, shift_row):
    center = values - jnp.mean(values, axis=-1, keepdims=True)
    spread = jnp.mean(center * center, axis=-1, keepdims=True)
    return center * lax.rsqrt(spread + 1e-05) * scale_row + shift_row


def normalize(key_rows):
    return key_rows * lax.rsqrt(jnp.mean(key_rows * key_rows, axis=-1, keepdims=True) + 1e-06)


def smooth(values):
    return jax.nn.gelu(values, approximate=False)


def combine(outputs, logsums):
    highest = jnp.max(logsums, axis=0, keepdims=True)
    powers = jnp.exp(logsums - highest)
    shares = powers / jnp.sum(powers, axis=0, keepdims=True)
    return jnp.sum(shares[..., None] * outputs, axis=0)


def reorder(values, row_order):
    if values.ndim > row_order.ndim:
        return jnp.take_along_axis(values, row_order[..., None], axis=2)
    return jnp.take_along_axis(values, row_order, axis=2)


def to_peers(values, row_order, groups):
    arranged = reorder(values, row_order)
    extent = arranged.shape
    return arranged.reshape(extent[:2] + (groups, extent[2] // groups) + extent[3:])


def from_peers(values):
    extent = values.shape
    return values.reshape(extent[:2] + (extent[2] * extent[3],) + extent[4:])


def padded_peers(values, sort_back, groups):
    extent = values.shape
    filler = jnp.zeros(extent[:2] + (sort_back.shape[-1] - extent[2],) + extent[3:], values.dtype)
    return to_peers(jnp.concatenate([values, filler], axis=2), sort_back, groups)


def make_routing(buckets, row_count):
    groups = lax.axis_size("seq")
    position = lax.axis_index("seq")
    per_owner = row_count // SPAN
    capacity = 2 * (row_count // groups)
    rounds, heads = (buckets.shape[0], buckets.shape[1])
    owners = buckets // per_owner
    own = lax.dynamic_slice_in_dim(owners, position * row_count, row_count, axis=2)
    send_order = jnp.argsort(own, axis=-1, stable=True)
    send_back = jnp.argsort(send_order, axis=-1)
    peers = jnp.arange(groups, dtype=jnp.int32)
    counts = jnp.sum((own[..., None] == peers).astype(jnp.int32), axis=2)
    starts = jnp.cumsum(counts, axis=-1) - counts
    slots = jnp.arange(capacity, dtype=jnp.int32)
    take = jnp.minimum(starts[..., None] + slots, row_count - 1).reshape(
        rounds, heads, groups * capacity
    )
    send_rows = jnp.take_along_axis(send_order, take, axis=-1)
    owner_sorted = jnp.take_along_axis(own, send_order, axis=-1)
    flat_sorted = (
        owner_sorted * capacity
        + jnp.arange(row_count, dtype=jnp.int32)
        - jnp.take_along_axis(starts, owner_sorted, axis=-1)
    )
    token_slot = jnp.take_along_axis(flat_sorted, send_back, axis=-1)
    blocked = buckets.reshape(rounds, heads, groups, row_count)
    mine = blocked // per_owner == position
    picked = jnp.argsort(jnp.where(mine, 0, 1).astype(jnp.int32), axis=-1, stable=True)[
        ..., :capacity
    ]
    count_in = jnp.sum(mine.astype(jnp.int32), axis=-1)
    arrived = jnp.take_along_axis(blocked, picked, axis=-1)
    keys = jnp.where(slots < count_in[..., None], arrived, 1 << 30).reshape(
        rounds, heads, groups * capacity
    )
    sort_full = jnp.argsort(keys, axis=-1, stable=True)
    sort_order = sort_full[..., :row_count]
    sort_back = jnp.argsort(sort_full, axis=-1)
    return (send_rows, token_slot, sort_order, sort_back)


def model_sum(partial_sum):
    return lax.psum(partial_sum, "mp")


def model_sum_back(partial_sum):
    return lax.psum(partial_sum, "mp")


def project(normed_low, query_weight, value_weight, groups, routing):
    row_count = normed_low.shape[0]
    queries = jnp.dot(normed_low, query_weight, preferred_element_type=jnp.float32).astype(
        jnp.bfloat16
    )
    values = jnp.dot(normed_low, value_weight, preferred_element_type=jnp.float32).astype(
        jnp.bfloat16
    )
    token_rows = jnp.concatenate(
        [queries.reshape(row_count, -1, DH), values.reshape(row_count, -1, DH)], axis=-1
    )
    token_rows = token_rows.transpose(1, 0, 2)
    spread = jnp.broadcast_to(token_rows[None], (ROUNDS,) + token_rows.shape)
    return to_peers(spread, routing[0], groups)


def window_parts(sorted_rows, previous):
    extent = sorted_rows.shape
    flat_count = extent[0] * extent[1]
    width = extent[3]
    blocks = sorted_rows.reshape(flat_count, extent[2] // SPAN, SPAN, width)
    earlier = jnp.concatenate(
        [previous.reshape(flat_count, 1, SPAN, width), blocks[:, :-1]], axis=1
    )
    window = jnp.concatenate([blocks, earlier], axis=2)
    queries = blocks[..., :DH]
    keys_float = window[..., :DH].astype(jnp.float32)
    normed = normalize(keys_float).astype(jnp.bfloat16)
    scores = jnp.einsum(
        "bcid,bcjd->bcij", queries, normed, preferred_element_type=jnp.float32
    ) / math.sqrt(DH)
    diagonal = jnp.arange(SPAN)[:, None] == jnp.arange(2 * SPAN)[None, :]
    scores = jnp.where(diagonal, -1000000000.0, scores)
    return (queries, keys_float, normed, window[..., DH:], scores)


def attend_forward(sorted_rows, previous):
    queries, keys_float, normed, values, scores = window_parts(sorted_rows, previous)
    highest = jnp.max(scores, axis=-1, keepdims=True)
    powers = jnp.exp(scores - highest)
    summed = jnp.sum(powers, axis=-1, keepdims=True)
    weights = (powers / summed).astype(jnp.bfloat16)
    output = jnp.einsum("bcij,bcjd->bcid", weights, values, preferred_element_type=jnp.float32)
    extent = sorted_rows.shape
    return (output.reshape(extent[:3] + (DH,)), (highest + jnp.log(summed)).reshape(extent[:3]))


def attend_backward(sorted_rows, previous, logsum, output_grad, logsum_grad):
    queries, keys_float, normed, values, scores = window_parts(sorted_rows, previous)
    flat_count, block_count = (scores.shape[0], scores.shape[1])
    probability = jnp.exp(scores - logsum.reshape(flat_count, block_count, SPAN, 1))
    weights = probability.astype(jnp.bfloat16)
    block_grad = output_grad.reshape(flat_count, block_count, SPAN, DH)
    prob_grad = jnp.einsum(
        "bcid,bcjd->bcij", block_grad, values, preferred_element_type=jnp.float32
    )
    value_grad = jnp.einsum(
        "bcij,bcid->bcjd", weights, block_grad, preferred_element_type=jnp.float32
    )
    weighted = jnp.sum(probability * prob_grad, axis=-1, keepdims=True)
    score_grad = probability * (
        prob_grad - weighted + logsum_grad.reshape(flat_count, block_count, SPAN, 1)
    )
    score_grad = score_grad / math.sqrt(DH)
    query_grad = jnp.einsum(
        "bcij,bcjd->bcid", score_grad, normed.astype(jnp.float32), precision=precise
    )
    normed_grad = jnp.einsum(
        "bcij,bcid->bcjd", score_grad, queries.astype(jnp.float32), precision=precise
    )
    key_grad = jax.vjp(normalize, keys_float)[1](normed_grad)[0]
    window_grad = jnp.concatenate([key_grad, value_grad], axis=-1)
    own_grad = window_grad[:, :, :SPAN] + jnp.concatenate(
        [query_grad, jnp.zeros_like(query_grad)], axis=-1
    )
    earlier_grad = window_grad[:, :, SPAN:]
    own_grad = own_grad + jnp.concatenate(
        [earlier_grad[:, 1:], jnp.zeros_like(earlier_grad[:, :1])], axis=1
    )
    extent = sorted_rows.shape
    return (
        own_grad.reshape(extent),
        earlier_grad[:, 0].reshape(extent[0], extent[1], SPAN, extent[3]),
    )


def layer_forward(first_stream, second_stream, weights, buckets, groups):
    (
        query_weight,
        value_weight,
        mixing_weight,
        mixing_bias,
        expand_weight,
        expand_bias,
        shrink_weight,
        shrink_bias,
        attention_gain,
        attention_shift,
        forward_gain,
        forward_shift,
    ) = weights
    row_count = first_stream.shape[0]
    routing = make_routing(buckets, row_count)
    send_rows, token_slot, sort_order, sort_back = routing
    normed_low = layer_norm(second_stream, attention_gain, attention_shift).astype(jnp.bfloat16)
    arrived = lax.all_to_all(
        project(normed_low, query_weight, value_weight, groups, routing),
        "seq",
        split_axis=2,
        concat_axis=2,
        tiled=True,
    )
    sorted_rows = reorder(from_peers(arrived), sort_order)
    previous = passed_along(sorted_rows[:, :, -SPAN:], "seq", 1)
    output, logsum = attend_forward(sorted_rows, previous)
    returned = (
        lax.all_to_all(
            padded_peers(output, sort_back, groups), "seq", split_axis=2, concat_axis=2, tiled=True
        ),
        lax.all_to_all(
            padded_peers(logsum, sort_back, groups), "seq", split_axis=2, concat_axis=2, tiled=True
        ),
    )
    outputs = reorder(from_peers(returned[0]), token_slot)
    logsums = reorder(from_peers(returned[1]), token_slot)
    combined_low = (
        combine(outputs, logsums).transpose(1, 0, 2).reshape(row_count, -1).astype(jnp.bfloat16)
    )
    mixed_stream = (
        first_stream
        + model_sum(jnp.dot(combined_low, mixing_weight, preferred_element_type=jnp.float32))
        + mixing_bias
    )
    normed_two = layer_norm(mixed_stream, forward_gain, forward_shift).astype(jnp.bfloat16)
    hidden = jnp.dot(normed_two, expand_weight, preferred_element_type=jnp.float32) + expand_bias
    active = smooth(hidden).astype(jnp.bfloat16)
    renewed = (
        second_stream
        + model_sum(jnp.dot(active, shrink_weight, preferred_element_type=jnp.float32))
        + shrink_bias
    )
    stored = (
        second_stream,
        mixed_stream,
        routing,
        normed_low,
        sorted_rows,
        previous,
        logsum,
        outputs,
        logsums,
        combined_low,
        normed_two,
        hidden,
        active,
    )
    return (mixed_stream, renewed, stored)


def layer_backward(first_grad, second_grad, weights, stored, groups):
    (
        query_weight,
        value_weight,
        mixing_weight,
        mixing_bias,
        expand_weight,
        expand_bias,
        shrink_weight,
        shrink_bias,
        attention_gain,
        attention_shift,
        forward_gain,
        forward_shift,
    ) = weights
    (
        second_stream,
        mixed_stream,
        routing,
        normed_low,
        sorted_rows,
        previous,
        logsum,
        outputs,
        logsums,
        combined_low,
        normed_two,
        hidden,
        active,
    ) = stored
    send_rows, token_slot, sort_order, sort_back = routing
    row_count = mixed_stream.shape[0]
    branch_grad = second_grad.astype(jnp.bfloat16)
    shrink_grad = jnp.einsum("tf,td->fd", active, branch_grad, preferred_element_type=jnp.float32)
    shrink_bias_grad = jnp.sum(branch_grad.astype(jnp.float32), axis=0)
    active_grad = jnp.einsum(
        "td,fd->tf", branch_grad, shrink_weight, preferred_element_type=jnp.float32
    )
    hidden_grad = jax.vjp(smooth, hidden)[1](active_grad)[0].astype(jnp.bfloat16)
    expand_grad = jnp.einsum(
        "td,tf->df", normed_two, hidden_grad, preferred_element_type=jnp.float32
    )
    expand_bias_grad = jnp.sum(hidden_grad.astype(jnp.float32), axis=0)
    two_grad = model_sum_back(
        jnp.einsum("tf,df->td", hidden_grad, expand_weight, preferred_element_type=jnp.float32)
    )
    norm_grads = jax.vjp(layer_norm, mixed_stream, forward_gain, forward_shift)[1](two_grad)
    mixed_grad = first_grad + norm_grads[0]
    mix_low = mixed_grad.astype(jnp.bfloat16)
    mixing_grad = jnp.einsum("th,td->hd", combined_low, mix_low, preferred_element_type=jnp.float32)
    mixing_bias_grad = jnp.sum(mix_low.astype(jnp.float32), axis=0)
    combined_grad = jnp.einsum(
        "td,hd->th", mix_low, mixing_weight, preferred_element_type=jnp.float32
    )
    combined_grad = combined_grad.reshape(row_count, -1, DH).transpose(1, 0, 2)
    outputs_grad, logsums_grad = jax.vjp(combine, outputs, logsums)[1](combined_grad)
    outputs_low = lax.optimization_barrier(outputs_grad.astype(jnp.bfloat16)).astype(jnp.float32)
    landed = (
        lax.all_to_all(
            to_peers(outputs_low, send_rows, groups), "seq", split_axis=2, concat_axis=2, tiled=True
        ),
        lax.all_to_all(
            to_peers(logsums_grad, send_rows, groups),
            "seq",
            split_axis=2,
            concat_axis=2,
            tiled=True,
        ),
    )
    sorted_grad = reorder(from_peers(landed[0]), sort_order).astype(jnp.bfloat16)
    sorted_lse_grad = reorder(from_peers(landed[1]), sort_order)
    arrived = lax.all_to_all(
        project(normed_low, query_weight, value_weight, groups, routing),
        "seq",
        split_axis=2,
        concat_axis=2,
        tiled=True,
    )
    sorted_rows = reorder(from_peers(arrived), sort_order)
    previous = passed_along(sorted_rows[:, :, -SPAN:], "seq", 1)
    rows_grad, halo_grad = attend_backward(
        sorted_rows, previous, logsum, sorted_grad, sorted_lse_grad
    )
    returned_halo = passed_along(halo_grad, "seq", -1)
    rows_grad = rows_grad.at[:, :, -SPAN:].add(returned_halo)
    homeward = lax.all_to_all(
        padded_peers(rows_grad, sort_back, groups), "seq", split_axis=2, concat_axis=2, tiled=True
    )
    merged = jnp.sum(reorder(from_peers(homeward), token_slot), axis=0).astype(jnp.bfloat16)
    query_grad = merged[..., :DH].transpose(1, 0, 2).reshape(row_count, -1)
    value_grad = merged[..., DH:].transpose(1, 0, 2).reshape(row_count, -1)
    query_weight_grad = jnp.einsum(
        "td,th->dh", normed_low, query_grad, preferred_element_type=jnp.float32
    )
    value_weight_grad = jnp.einsum(
        "td,th->dh", normed_low, value_grad, preferred_element_type=jnp.float32
    )
    one_grad = jnp.einsum("th,dh->td", query_grad, query_weight, preferred_element_type=jnp.float32)
    one_grad = model_sum_back(
        one_grad
        + jnp.einsum("th,dh->td", value_grad, value_weight, preferred_element_type=jnp.float32)
    )
    first_norm = jax.vjp(layer_norm, second_stream, attention_gain, attention_shift)[1](one_grad)
    gradients = [
        query_weight_grad,
        value_weight_grad,
        mixing_grad,
        mixing_bias_grad,
        expand_grad,
        expand_bias_grad,
        shrink_grad,
        shrink_bias_grad,
        first_norm[1],
        first_norm[2],
        norm_grads[1],
        norm_grads[2],
    ]
    return (mixed_grad, second_grad + first_norm[0], gradients)


def shards(
    stream_one,
    stream_two,
    cotangent_one,
    cotangent_two,
    bucket_numbers,
    query_weight,
    value_weight,
    mixing_weight,
    mixing_bias,
    expand_weight,
    expand_bias,
    shrink_weight,
    shrink_bias,
    attention_gain,
    attention_shift,
    forward_gain,
    forward_shift,
):
    groups = lax.axis_size("seq")
    params = (
        query_weight,
        value_weight,
        mixing_weight,
        mixing_bias,
        expand_weight,
        expand_bias,
        shrink_weight,
        shrink_bias,
        attention_gain,
        attention_shift,
        forward_gain,
        forward_shift,
    )
    first_stream, second_stream = (stream_one, stream_two)
    saved_layers = []
    for number in range(LAYERS):
        layer_weights = tuple((member[number] for member in params))
        first_stream, second_stream, stored = layer_forward(
            first_stream, second_stream, layer_weights, bucket_numbers[number], groups
        )
        saved_layers.append(stored)
    first_grad, second_grad = (cotangent_one, cotangent_two)
    collected = [None] * LAYERS
    for number in reversed(range(LAYERS)):
        layer_weights = tuple((member[number] for member in params))
        first_grad, second_grad, gradients = layer_backward(
            first_grad, second_grad, layer_weights, saved_layers[number], groups
        )
        collected[number] = gradients
    stacked = [
        jnp.stack([collected[number][member_index] for number in range(LAYERS)])
        for member_index in range(12)
    ]
    stacked = list(
        (
            lax.psum_scatter(stacked[0], "seq", scatter_dimension=1, tiled=True),
            lax.psum_scatter(stacked[1], "seq", scatter_dimension=1, tiled=True),
            lax.psum_scatter(stacked[2], "seq", scatter_dimension=1, tiled=True),
            lax.psum_scatter(stacked[3], "seq", scatter_dimension=1, tiled=True),
            lax.psum_scatter(stacked[4], "seq", scatter_dimension=1, tiled=True),
            lax.psum_scatter(stacked[5], "seq", scatter_dimension=1, tiled=True),
            lax.psum_scatter(stacked[6], "seq", scatter_dimension=1, tiled=True),
            lax.psum_scatter(stacked[7], "seq", scatter_dimension=1, tiled=True),
            lax.psum_scatter(stacked[8], "seq", scatter_dimension=1, tiled=True),
            lax.psum_scatter(stacked[9], "seq", scatter_dimension=1, tiled=True),
            lax.psum_scatter(stacked[10], "seq", scatter_dimension=1, tiled=True),
            lax.psum_scatter(stacked[11], "seq", scatter_dimension=1, tiled=True),
        )
    )
    return (
        first_stream,
        second_stream,
        first_grad,
        second_grad,
        stacked[0],
        stacked[1],
        stacked[2],
        stacked[3],
        stacked[4],
        stacked[5],
        stacked[6],
        stacked[7],
        stacked[8],
        stacked[9],
        stacked[10],
        stacked[11],
    )


def solution(mesh):
    in_specs = (
        P("seq", None),
        P("seq", None),
        P("seq", None),
        P("seq", None),
        P(None, None, "mp", None),
        P(None, None, "mp"),
        P(None, None, "mp"),
        P(None, "mp", None),
        P(),
        P(None, None, "mp"),
        P(None, "mp"),
        P(None, "mp", None),
        P(),
        P(),
        P(),
        P(),
        P(),
    )
    out_specs = (
        P("seq", None),
        P("seq", None),
        P("seq", None),
        P("seq", None),
        P(None, "seq", "mp"),
        P(None, "seq", "mp"),
        P(None, ("mp", "seq"), None),
        P(None, "seq"),
        P(None, "seq", "mp"),
        P(None, ("mp", "seq")),
        P(None, ("mp", "seq"), None),
        P(None, "seq"),
        P(None, "seq"),
        P(None, "seq"),
        P(None, "seq"),
        P(None, "seq"),
    )
    return jax.shard_map(shards, mesh=mesh, in_specs=in_specs, out_specs=out_specs, check_vma=False)
```

profile of v0, /device:TPU:0, one launch (start us, length us, event | category | flops | bytes accessed | tf_op | source)
XLA Modules:
  0.0 2917.4 jit_solution(7489629963473093901)
XLA Ops:
  92.2 45.6 %gather_fusion.1 = bf16[4096,256]{1,0:T(8,128)(2,1)} fusion(bf16[4,4,128,256]{3,2,1,0:T(8,128)(2,1)S(1)} %broadcast_in_dim.144, s32[4096]{0:T(1024)S(1)} %bitcast.491), kind=kCustom, calls=%fused_computation.1.clone | custom fusion | bytes 4243456 | tf_op jit(solution)/shard_map/jit(take_along_axis)/gather | solution.py:46
  179.6 39.6 %gather_fusion.2 = s32[4096]{0:T(1024)S(1)} fusion(s32[4,4,16,128]{3,2,1,0:T(8,128)S(1)} %reshape_squeeze.12, s32[4096]{0:T(1024)S(1)} %reshape.953), kind=kCustom, calls=%fused_computation.2.clone | custom fusion | bytes 98304 | tf_op jit(solution)/shard_map/jit(take_along_axis)/gather | solution.py:98
  276.3 40.3 %gather_fusion.4 = f32[4096]{0:T(1024)S(1)} fusion(f32[4,4,256]{2,1,0:T(4,128)S(1)} %concatenate.67, s32[4096]{0:T(1024)S(1)} %bitcast.507), kind=kCustom, calls=%fused_computation.4.clone | custom fusion | bytes 81920 | tf_op jit(solution)/shard_map/jit(take_along_axis)/gather | solution.py:47
  321.1 51.1 %gather_fusion.9 = f32[4096,128]{1,0:T(8,128)} fusion(f32[4,4,256,128]{3,2,1,0:T(8,128)S(1)} %concatenate.68, s32[4096]{0:T(1024)S(1)} %bitcast.487), kind=kCustom, calls=%fused_computation.8.clone | custom fusion | bytes 4243456 | tf_op jit(solution)/shard_map/jit(take_along_axis)/gather | solution.py:46
  572.6 45.6 %gather_fusion.12 = bf16[4096,256]{1,0:T(8,128)(2,1)} fusion(bf16[4,4,128,256]{3,2,1,0:T(8,128)(2,1)S(1)} %broadcast_in_dim.150, s32[4096]{0:T(1024)S(1)} %bitcast.493), kind=kCustom, calls=%fused_computation.15.clone | custom fusion | bytes 4243456 | tf_op jit(solution)/shard_map/jit(take_along_axis)/gather | solution.py:46
  658.3 39.6 %gather_fusion.13 = s32[4096]{0:T(1024)S(1)} fusion(s32[4,4,16,128]{3,2,1,0:T(8,128)S(1)} %reshape_squeeze.13, s32[4096]{0:T(1024)S(1)} %reshape.1004), kind=kCustom, calls=%fused_computation.16.clone | custom fusion | bytes 98304 | tf_op jit(solution)/shard_map/jit(take_along_axis)/gather | solution.py:98
  751.2 40.3 %gather_fusion.15 = f32[4096]{0:T(1024)S(1)} fusion(f32[4,4,256]{2,1,0:T(4,128)S(1)} %concatenate.72, s32[4096]{0:T(1024)S(1)} %bitcast.506), kind=kCustom, calls=%fused_computation.18.clone | custom fusion | bytes 81920 | tf_op jit(solution)/shard_map/jit(take_along_axis)/gather | solution.py:47
  796.4 51.1 %gather_fusion.20 = f32[4096,128]{1,0:T(8,128)} fusion(f32[4,4,256,128]{3,2,1,0:T(8,128)S(1)} %concatenate.73, s32[4096]{0:T(1024)S(1)} %bitcast.489), kind=kCustom, calls=%fused_computation.26.clone | custom fusion | bytes 4243456 | tf_op jit(solution)/shard_map/jit(take_along_axis)/gather | solution.py:46
  1210.5 70.0 %gather_fusion.26 = f32[4096,256]{1,0:T(8,128)} fusion(f32[4,4,256,256]{3,2,1,0:T(8,128)} %concatenate.77, s32[4096]{0:T(1024)S(1)} %bitcast.490), kind=kCustom, calls=%fused_computation.12.clone | custom fusion | bytes 8437760 | tf_op jit(solution)/shard_map/jit(take_along_axis)/gather | solution.py:46
  1284.4 98.5 %all_to_all.62 = f32[4,4,16,16,256]{4,3,1,0,2:T(8,128)S(1)} all-to-all(f32[4,4,16,16,256]{4,3,1,0,2:T(8,128)S(1)} %copy.222), channel_id=1, replica_groups=mesh['seq'=16,'mp'=2] {'seq'}, dimensions={2} | all-to-all | bytes 8388608 | tf_op jit(solution)/shard_map/all_to_all | solution.py:360
  1655.8 70.0 %gather_fusion.32 = f32[4096,256]{1,0:T(8,128)} fusion(f32[4,4,256,256]{3,2,1,0:T(8,128)} %concatenate.81, s32[4096]{0:T(1024)S(1)} %bitcast.488), kind=kCustom, calls=%fused_computation.32.clone | custom fusion | bytes 8437760 | tf_op jit(solution)/shard_map/jit(take_along_axis)/gather | solution.py:46
  1743.5 72.0 %all-to-all-done.11 = f32[4,4,16,16,256]{4,3,1,0,2:T(8,128)} async-done(((f32[4,4,16,16,256]{4,3,1,0,2:T(8,128)}), f32[4,4,16,16,256]{4,3,1,0,2:T(8,128)}, u32[]{:S(2)}, u32[]{:S(2)}) %all-to-all-start.11) | async-done | bytes 4194336 | tf_op jit(solution)/shard_map/all_to_all | solution.py:360
  1856.9 47.3 %all-reduce.31.cloned.1.call-done = (f32[128,1024]{1,0:T(8,128)}, f32[128,1024]{1,0:T(8,128)}) async-done(((f32[128,1024]{1,0:T(8,128)}, f32[128,1024]{1,0:T(8,128)}), (f32[128,1024]{1,0:T(8,128)}, f32[128,1024]{1,0:T(8,128)})) %all-reduce.31.cloned.1.call-update) | async-done | bytes 1048592 | tf_op jit(solution)/shard_map/psum | solution.py:109
  1967.0 56.9 %reduce-scatter.37.cloned.1.call-done = f32[64,2]{1,0:T(8,128)} async-done(((f32[1024,2]{1,0:T(8,128)}), f32[64,2]{1,0:T(8,128)}) %reduce-scatter.37.cloned.1.call-update) | async-done | bytes 528
  2025.3 57.3 %reduce-scatter.47.cloned.1.call-done = f32[64,2]{1,0:T(8,128)} async-done(((f32[1024,2]{1,0:T(8,128)}), f32[64,2]{1,0:T(8,128)}) %reduce-scatter.47.cloned.1.call-update) | async-done | bytes 528
  2084.0 57.0 %reduce-scatter.49.cloned.1.call-done = f32[64,2]{1,0:T(8,128)} async-done(((f32[1024,2]{1,0:T(8,128)}), f32[64,2]{1,0:T(8,128)}) %reduce-scatter.49.cloned.1.call-update) | async-done | bytes 528
  2143.2 56.5 %reduce-scatter.41.cloned.1.call-done = f32[64,2]{1,0:T(8,128)} async-done(((f32[1024,2]{1,0:T(8,128)}), f32[64,2]{1,0:T(8,128)}) %reduce-scatter.41.cloned.1.call-update) | async-done | bytes 528
  2201.1 57.0 %reduce-scatter.43.cloned.1.call-done = f32[64,2]{1,0:T(8,128)} async-done(((f32[1024,2]{1,0:T(8,128)}), f32[64,2]{1,0:T(8,128)}) %reduce-scatter.43.cloned.1.call-update) | async-done | bytes 528
  2259.6 57.3 %reduce-scatter.45.cloned.1.call-done = f32[64,2]{1,0:T(8,128)} async-done(((f32[1024,2]{1,0:T(8,128)}), f32[64,2]{1,0:T(8,128)}) %reduce-scatter.45.cloned.1.call-update) | async-done | bytes 528
  2318.3 74.5 %reduce-scatter.31.cloned.1.call-done = f32[2,32,1024]{2,1,0:T(8,128)} async-done(((f32[2,512,1024]{2,1,0:T(8,128)}), f32[2,32,1024]{2,1,0:T(8,128)}) %reduce-scatter.31.cloned.1.call-update) | async-done | bytes 262160 | tf_op jit(solution)/shard_map/reduce_scatter | solution.py:453
  2392.8 76.2 %reduce-scatter.27.cloned.1.call-done = f32[2,64,512]{2,1,0:T(8,128)} async-done(((f32[2,1024,512]{2,1,0:T(8,128)}), f32[2,64,512]{2,1,0:T(8,128)}) %reduce-scatter.27.cloned.1.call-update) | async-done | bytes 262160 | tf_op jit(solution)/shard_map/reduce_scatter | solution.py:451
  2469.0 75.9 %reduce-scatter.29.cloned.1.call-done = f32[2,64,512]{2,1,0:T(8,128)} async-done(((f32[2,1024,512]{2,1,0:T(8,128)}), f32[2,64,512]{2,1,0:T(8,128)}) %reduce-scatter.29.cloned.1.call-update) | async-done | bytes 262160 | tf_op jit(solution)/shard_map/reduce_scatter | solution.py:452
  2544.8 182.8 %reduce-scatter.33.cloned.1.call-done = f32[2,64,2048]{2,1,0:T(8,128)} async-done(((f32[2,1024,2048]{2,1,0:T(8,128)}), f32[2,64,2048]{2,1,0:T(8,128)}) %reduce-scatter.33.cloned.1.call-update) | async-done | bytes 1048592 | tf_op jit(solution)/shard_map/reduce_scatter | solution.py:455
  2727.6 182.8 %reduce-scatter.35.cloned.1.call-done = f32[2,128,1024]{2,1,0:T(8,128)} async-done(((f32[2,2048,1024]{2,1,0:T(8,128)}), f32[2,128,1024]{2,1,0:T(8,128)}) %reduce-scatter.35.cloned.1.call-update) | async-done | bytes 1048592 | tf_op jit(solution)/shard_map/reduce_scatter | solution.py:457
  (809 shorter events, 1253.8 us)
Async XLA Ops:
  141.4 90.7 %all-to-all-start = ((bf16[4,4,16,16,256]{4,3,1,0,2:T(8,128)(2,1)}), bf16[4,4,16,16,256]{4,3,1,0,2:T(8,128)(2,1)}, u32[]{:S(2)}, u32[]{:S(2)}) async-start(bf16[4,4,16,16,256]{4,3,1,0,2:T(8,128)(2,1)} %copy.194), calls=%async_computation | async-start | bytes 4194304 | tf_op jit(solution)/shard_map/all_to_all | solution.py:221
  375.9 91.2 %all-to-all-start.2 = ((f32[4,4,16,16,128]{4,3,1,0,2:T(8,128)}), f32[4,4,16,16,128]{4,3,1,0,2:T(8,128)}, u32[]{:S(2)}, u32[]{:S(2)}) async-start(f32[4,4,16,16,128]{4,3,1,0,2:T(8,128)} %copy.200), calls=%async_computation.2 | async-start | bytes 4194304 | tf_op jit(solution)/shard_map/all_to_all | solution.py:232
  421.4 108.0 %all-reduce.19.cloned.1.call-start = ((), (), s32[]{:S(2)}) async-start(), calls=%async_computation.24 | async-start | bytes 1048576 | tf_op jit(solution)/shard_map/psum | solution.py:109
  499.3 69.1 %all-reduce.21.cloned.1.call-start = ((), (), s32[]{:S(2)}) async-start(), calls=%async_computation.25 | async-start | bytes 1048576 | tf_op jit(solution)/shard_map/psum | solution.py:109
  621.8 87.7 %all-to-all-start.3 = ((bf16[4,4,16,16,256]{4,3,1,0,2:T(8,128)(2,1)}), bf16[4,4,16,16,256]{4,3,1,0,2:T(8,128)(2,1)}, u32[]{:S(2)}, u32[]{:S(2)}) async-start(bf16[4,4,16,16,256]{4,3,1,0,2:T(8,128)(2,1)} %copy.204), calls=%async_computation.3 | async-start | bytes 4194304 | tf_op jit(solution)/shard_map/all_to_all | solution.py:221
  851.1 91.3 %all-to-all-start.5 = ((f32[4,4,16,16,128]{4,3,1,0,2:T(8,128)}), f32[4,4,16,16,128]{4,3,1,0,2:T(8,128)}, u32[]{:S(2)}, u32[]{:S(2)}) async-start(f32[4,4,16,16,128]{4,3,1,0,2:T(8,128)} %copy.210), calls=%async_computation.5 | async-start | bytes 4194304 | tf_op jit(solution)/shard_map/all_to_all | solution.py:232
  897.3 106.4 %all-reduce.23.cloned.1.call-start = ((), (), s32[]{:S(2)}) async-start(), calls=%async_computation.26 | async-start | bytes 1048576 | tf_op jit(solution)/shard_map/psum | solution.py:109
  974.6 71.8 %all-reduce.25.cloned.1.call-start = ((), (), s32[]{:S(2)}) async-start(), calls=%async_computation.27 | async-start | bytes 1048576 | tf_op jit(solution)/shard_map/psum | solution.py:113
  1130.8 316.2 %all-reduce.27.cloned.1.call-start = ((), (), s32[]{:S(2)}) async-start(), calls=%async_computation.28 | async-start | bytes 1048576 | tf_op jit(solution)/shard_map/psum | solution.py:113
  1418.6 72.1 %all-reduce.29.cloned.1.call-start = ((), (), s32[]{:S(2)}) async-start(), calls=%async_computation.29 | async-start | bytes 1048576 | tf_op jit(solution)/shard_map/psum | solution.py:113
  1731.7 83.8 %all-to-all-start.11 = ((f32[4,4,16,16,256]{4,3,1,0,2:T(8,128)}), f32[4,4,16,16,256]{4,3,1,0,2:T(8,128)}, u32[]{:S(2)}, u32[]{:S(2)}) async-start(f32[4,4,16,16,256]{4,3,1,0,2:T(8,128)} %copy.235), calls=%async_computation.11 | async-start | bytes 8388608 | tf_op jit(solution)/shard_map/all_to_all | solution.py:360
  1737.9 166.3 %all-reduce.31.cloned.1.call-start = ((), (), s32[]{:S(2)}) async-start(), calls=%async_computation.42 | async-start | bytes 2097152 | tf_op jit(solution)/shard_map/psum | solution.py:109
  1849.7 115.8 %reduce-scatter.39.cloned.1.call-start = ((), (), s32[]{:S(2)}) async-start(), calls=%async_computation.36 | async-start | bytes 1114112
  1851.6 172.2 %reduce-scatter.37.cloned.1.call-start = ((), (), s32[]{:S(2)}) async-start(), calls=%async_computation.35 | async-start | bytes 557056
  1854.6 228.0 %reduce-scatter.47.cloned.1.call-start = ((), (), s32[]{:S(2)}) async-start(), calls=%async_computation.40 | async-start | bytes 557056
  1855.7 285.2 %reduce-scatter.49.cloned.1.call-start = ((), (), s32[]{:S(2)}) async-start(), calls=%async_computation.41 | async-start | bytes 557056
  1856.9 342.9 %reduce-scatter.41.cloned.1.call-start = ((), (), s32[]{:S(2)}) async-start(), calls=%async_computation.37 | async-start | bytes 557056
  1909.0 349.2 %reduce-scatter.43.cloned.1.call-start = ((), (), s32[]{:S(2)}) async-start(), calls=%async_computation.38 | async-start | bytes 557056
  1910.1 406.8 %reduce-scatter.45.cloned.1.call-start = ((), (), s32[]{:S(2)}) async-start(), calls=%async_computation.39 | async-start | bytes 557056
  1911.2 481.6 %reduce-scatter.31.cloned.1.call-start = ((), (), s32[]{:S(2)}) async-start(), calls=%async_computation.32 | async-start | bytes 4456448 | tf_op jit(solution)/shard_map/reduce_scatter | solution.py:453
  1915.5 553.5 %reduce-scatter.27.cloned.1.call-start = ((), (), s32[]{:S(2)}) async-start(), calls=%async_computation.30 | async-start | bytes 4456448 | tf_op jit(solution)/shard_map/reduce_scatter | solution.py:451
  1919.8 625.0 %reduce-scatter.29.cloned.1.call-start = ((), (), s32[]{:S(2)}) async-start(), calls=%async_computation.31 | async-start | bytes 4456448 | tf_op jit(solution)/shard_map/reduce_scatter | solution.py:452
  1924.2 803.5 %reduce-scatter.33.cloned.1.call-start = ((), (), s32[]{:S(2)}) async-start(), calls=%async_computation.33 | async-start | bytes 17825792 | tf_op jit(solution)/shard_map/reduce_scatter | solution.py:455
  1934.2 976.3 %reduce-scatter.35.cloned.1.call-start = ((), (), s32[]{:S(2)}) async-start(), calls=%async_computation.34 | async-start | bytes 17825792 | tf_op jit(solution)/shard_map/reduce_scatter | solution.py:457
  (186 other events, 6144.2 us)
Sparse Core Ops, SparseCore 0:
  152.6 25.7 sort.168.cloned.1.call-done
  220.9 8.1 sort.170.cloned.1.call-done
  499.5 29.8 all-reduce.18
  539.8 28.5 all-reduce.20
  631.2 25.7 sort.178.cloned.1.call-done
  699.6 8.1 sort.180.cloned.1.call-done
  737.0 4.4 sort.182.cloned.1.call-done
  974.7 28.9 all-reduce.22
  1017.8 28.5 all-reduce.24
  1418.7 28.2 all-reduce.26
  1462.1 28.5 all-reduce.28
  1849.8 54.3 all-reduce.30
  1908.1 57.3 reduce-scatter.38
  1969.1 54.7 reduce-scatter.36
  2027.7 54.8 reduce-scatter.46
  2086.1 54.7 reduce-scatter.48
  2144.9 54.7 reduce-scatter.40
  2203.3 54.8 reduce-scatter.42
  2262.0 54.8 reduce-scatter.44
  2321.3 71.4 reduce-scatter.30
  2397.6 71.3 reduce-scatter.26
  2473.2 71.5 reduce-scatter.28
  2550.1 177.5 reduce-scatter.32
  2732.9 177.5 reduce-scatter.34
  (15 shorter events, 18.1 us)
where the time goes:
time: 2930 us; the launch traced here: 2920 us
  waiting for transfers between devices  1290 us (44%)
  local copies, waits for them, and re-layouts  1250 us (43%)
  other arithmetic  110 us (4%)
  blocking collectives  98.5 us (3%)
  matrix products  81 us (3%)
  starting transfers between devices  70.7 us (2%)
    gather x16, local copies, waits for them, and re-layouts, reorder(): return jnp.take_along_axis(values, row_order[..., None], axis=2)  580 us
    unnamed x26, waiting for transfers between devices  360 us
    gather x12, local copies, waits for them, and re-layouts, reorder(): return jnp.take_along_axis(values, row_order, axis=2)  236 us
    reduce_scatter x1, waiting for transfers between devices, shards(): lax.psum_scatter(stacked[6], 'seq', scatter_dimension=1, tiled=True)  183 us
    reduce_scatter x1, waiting for transfers between devices, shards(): lax.psum_scatter(stacked[4], 'seq', scatter_dimension=1, tiled=True)  183 us
    psum x4, waiting for transfers between devices, model_sum(): return lax.psum(partial_sum, 'mp')  134 us
    all_to_all x1, blocking collectives, layer_backward(): lax.all_to_all(padded_peers(rows_grad, sort_back, groups), 'seq', split_a...  98.5 us
    psum x3, waiting for transfers between devices, model_sum_back(): return lax.psum(partial_sum, 'mp')  84.2 us
  transfers between devices with their start and end apart: 34, of which 28 were waited for; matrix products, arithmetic and copies ran while one was open for 16% of the time, Pallas kernels for 0%

commit v1 on v0

v1 whole, which is shorter than its diff:
```python
import functools
import math
from types import SimpleNamespace
from typing import NamedTuple

import jax
import jax.numpy as jnp
from jax import lax
from jax.experimental import pallas as pl
from jax.experimental.pallas import tpu as pltpu
from jax.sharding import PartitionSpec as P

DH = 128
SPAN = 64
ROUNDS = 4
LAYERS = 2
LANES = 128
CHUNK = 128
MESH = pl.DeviceIdType.MESH
F32 = jnp.float32
BF16 = jnp.bfloat16
AWAY = -1e30
VMEM_LIMIT = 60 << 20


class Sizes(NamedTuple):
    seq: int
    tok: int
    heads: int
    plane: int
    bits: int
    parts: int
    total: int
    rows: int
    ext: int
    buckets: int
    feats: int
    width: int
    hid: int


def sizes_of(seq, stream, query_weight, expand_weight):
    tok, feats = stream.shape
    width = query_weight.shape[2]
    heads = width // DH
    plane = seq // heads
    parts = plane // ROUNDS
    total = seq * tok
    rows = total // parts
    return Sizes(
        seq,
        tok,
        heads,
        plane,
        plane.bit_length() - 1,
        parts,
        total,
        rows,
        rows + CHUNK,
        total // SPAN,
        feats,
        width,
        expand_weight.shape[2],
    )


def dot(left, right):
    return lax.dot_general(left, right, (((1,), (0,)), ((), ())), preferred_element_type=F32)


def dot_nt(left, right):
    return lax.dot_general(left, right, (((1,), (1,)), ((), ())), preferred_element_type=F32)


def dot_tn(left, right):
    return lax.dot_general(left, right, (((0,), (0,)), ((), ())), preferred_element_type=F32)


def norm_parts(values):
    center = values - jnp.mean(values, axis=-1, keepdims=True)
    scale = lax.rsqrt(jnp.mean(center * center, axis=-1, keepdims=True) + 1e-05)
    return center * scale, scale


def norm_back(xhat, scale, gain, grad):
    t = grad * gain
    inner = t - jnp.mean(t, axis=-1, keepdims=True) - xhat * jnp.mean(t * xhat, axis=-1, keepdims=True)
    return scale * inner


def key_scale(keys):
    return lax.rsqrt(jnp.mean(keys * keys, axis=-1, keepdims=True) + 1e-06)


def rows_to_columns(rows):
    return jnp.transpose(jnp.broadcast_to(rows, (LANES, rows.shape[1])))


def split_three(values):
    high = values.astype(BF16).astype(F32)
    rest = values - high
    middle = rest.astype(BF16).astype(F32)
    return high, middle, rest - middle


class Place:
    def __init__(self, cfg):
        self.cfg = cfg
        self.index = lax.axis_index("seq")
        self.half = lax.axis_index("mp")
        self.head = self.index // cfg.plane
        self.member = self.index % cfg.plane
        self.round = self.member // cfg.parts
        self.part = self.member % cfg.parts

    def bit(self, k):
        return (self.member // 2**k) % 2

    def z_peer(self, step):
        head = (self.head + step) % self.cfg.heads
        return head, (head * self.cfg.plane + self.member, self.half)

    def z_source(self, step):
        return (self.head + self.cfg.heads - step) % self.cfg.heads

    def bit_peer(self, k):
        return (self.index + (1 - 2 * self.bit(k)) * 2**k, self.half)

    def y_peer(self):
        return (self.index, 1 - self.half)

    def kept(self, k, i):
        return 2 ** (k + 1) * i + self.member % 2 ** (k + 1)

    def given(self, k, i):
        return 2 ** (k + 1) * i + (1 - self.bit(k)) * 2**k + self.member % 2**k

    def group(self, k):
        return self.cfg.plane // 2 ** (k + 1)

    def greet(self):
        barrier = pltpu.get_barrier_semaphore()
        peers = [self.z_peer(step)[1] for step in range(1, self.cfg.heads)]
        peers += [self.bit_peer(k) for k in range(self.cfg.bits)]
        peers += [self.y_peer()]
        for peer in peers:
            pl.semaphore_signal(barrier, inc=1, device_id=peer, device_id_type=MESH)
        pl.semaphore_wait(barrier, len(peers))


def remote(src, dst, send, recv, peer):
    return pltpu.make_async_remote_copy(
        src_ref=src, dst_ref=dst, send_sem=send, recv_sem=recv, device_id=peer, device_id_type=MESH
    )


def rank_rows(cfg, bucket_row, rank_ref):
    count = cfg.buckets
    ids = lax.broadcasted_iota(jnp.int32, (count, LANES), 0)
    ahead = (
        lax.broadcasted_iota(jnp.int32, (LANES, LANES), 0)
        < lax.broadcasted_iota(jnp.int32, (LANES, LANES), 1)
    ).astype(BF16)
    lower = (
        lax.broadcasted_iota(jnp.int32, (count, count), 1)
        < lax.broadcasted_iota(jnp.int32, (count, count), 0)
    ).astype(BF16)
    marks = [
        (bucket_row[:, p * LANES : (p + 1) * LANES] == ids).astype(F32) for p in range(cfg.seq)
    ]
    totals = sum(marks)
    totals = jnp.broadcast_to(jnp.sum(totals, axis=1, keepdims=True), (count, LANES))
    carry = dot(lower, totals.astype(BF16))
    for p in range(cfg.seq):
        within = dot(marks[p].astype(BF16), ahead)
        rank = jnp.sum(marks[p] * (within + carry), axis=0, keepdims=True)
        carry = carry + jnp.broadcast_to(jnp.sum(marks[p], axis=1, keepdims=True), (count, LANES))
        spot = (p % cfg.plane) * cfg.heads + p // cfg.plane
        rank_ref[:, spot * LANES : (spot + 1) * LANES] = jnp.broadcast_to(
            rank.astype(jnp.int32), (8, LANES)
        )


def sort_rows(cfg, rank_ref, source_ref, store, start, size, chunks):
    step = min(cfg.total, 2048)

    def body(c, _):
        spots = start + c * size + lax.broadcasted_iota(jnp.int32, (size, step), 0)
        spots = spots % cfg.total if cfg.parts > 1 else spots
        found = None
        for k in range(cfg.total // step):
            ranks = rank_ref[0:1, k * step : (k + 1) * step]
            pick = (spots == ranks).astype(BF16)
            part = dot(pick, source_ref[k * step : (k + 1) * step, :])
            found = part if found is None else found + part
        store(c, found)
        return 0

    lax.fori_loop(0, chunks, body, 0)


def window_mask():
    row = lax.broadcasted_iota(jnp.int32, (CHUNK, 2 * CHUNK), 0)
    column = lax.broadcasted_iota(jnp.int32, (CHUNK, 2 * CHUNK), 1)
    gap = column // SPAN - row // SPAN
    near = jnp.logical_or(gap == 1, gap == 2)
    return jnp.logical_and(near, column != row + CHUNK)


def z_exchange(cfg, place, source, target, send, recv):
    copies = []
    for step in range(1, cfg.heads):
        head, peer = place.z_peer(step)
        copy = remote(source(head), target(place.head), send.at[step], recv.at[step], peer)
        copy.start()
        copies.append(copy)
    return copies


def z_arrival(place, block, recv, step):
    return remote(block, block, recv.at[step], recv.at[step], place.z_peer(step)[1])


class Doubling:
    def __init__(self, place, keys, block, send, recv):
        self.place, self.keys, self.block = place, keys, block
        self.send, self.recv = send, recv

    def give(self, key, spot, k):
        return remote(
            self.block(key, spot),
            self.block(key, spot),
            self.send.at[k, key, spot],
            self.recv.at[key, spot],
            self.place.bit_peer(k),
        )

    def offer(self, key):
        for k in range(self.place.cfg.bits):
            self.give(key, self.place.member, k).start()

    def spots(self):
        for k in reversed(range(self.place.cfg.bits)):
            for key in self.keys:
                for i in range(self.place.group(k)):
                    yield k, key, self.place.given(k, i)

    def receive(self):
        for k, key, spot in self.spots():
            self.give(key, spot, k).wait_recv()
            for low in range(k):
                self.give(key, spot, low).start()

    def finish(self):
        for key in self.keys:
            for k in range(self.place.cfg.bits):
                self.give(key, self.place.member, k).wait_send()
        for k, key, spot in self.spots():
            for low in range(k):
                self.give(key, spot, low).wait_send()


class Params(NamedTuple):
    wq_hbm: jax.Array
    wv_hbm: jax.Array
    wm_hbm: jax.Array
    mix_bias: jax.Array
    we_hbm: jax.Array
    expand_bias: jax.Array
    ws_hbm: jax.Array
    shrink_bias: jax.Array
    attention_gain: jax.Array
    attention_shift: jax.Array
    forward_gain: jax.Array
    forward_shift: jax.Array


class Streams(NamedTuple):
    first: jax.Array
    second: jax.Array
    buckets: jax.Array


class Kept(NamedTuple):
    mixed: jax.Array
    sorted: jax.Array
    comb: jax.Array
    joint: jax.Array
    hidden: jax.Array
    rank: jax.Array
    normed_t: jax.Array
    normed_two_t: jax.Array
    active_t: jax.Array
    low_t: jax.Array
    second: jax.Array


class Grads(NamedTuple):
    first_out: jax.Array
    second_out: jax.Array
    out_wq: jax.Array
    out_wv: jax.Array
    out_wm: jax.Array
    out_we: jax.Array
    out_ws: jax.Array
    out_small: jax.Array


def gathered(*groups, **scratch):
    merged = {}
    for group in groups:
        merged.update(group._asdict())
    return SimpleNamespace(**merged, **scratch)


def forward_scratch(cfg):
    tok, heads, plane, bits = cfg.tok, cfg.heads, cfg.plane, cfg.bits
    band = heads * tok
    dma = pltpu.SemaphoreType.DMA
    return dict(
        wq=pltpu.VMEM((cfg.feats, cfg.width), BF16),
        wv=pltpu.VMEM((cfg.feats, cfg.width), BF16),
        wm=pltpu.VMEM((cfg.width, cfg.feats), BF16),
        we=pltpu.VMEM((cfg.feats, cfg.hid), BF16),
        ws=pltpu.VMEM((cfg.hid, cfg.feats), BF16),
        zs=pltpu.VMEM((heads, tok, 2 * DH), BF16),
        tokens=pltpu.VMEM((cfg.total, 2 * DH), BF16),
        keys=pltpu.VMEM((cfg.ext, DH), BF16),
        attended=pltpu.VMEM((cfg.rows, 3 * DH), BF16),
        part=pltpu.VMEM((plane, band, DH), F32),
        lrow=pltpu.VMEM((plane, 8, band), F32),
        part_in=pltpu.VMEM((bits, plane, band, DH), F32),
        lrow_in=pltpu.VMEM((bits, plane, 8, band), F32),
        low_out=pltpu.VMEM((heads, tok, DH), BF16),
        low_in=pltpu.VMEM((heads, tok, DH), BF16),
        ys=pltpu.VMEM((2, tok, cfg.feats), BF16),
        yr=pltpu.VMEM((2, tok, cfg.feats), BF16),
        wsem=dma((5,)),
        zsend=dma((heads,)),
        zrecv=dma((heads,)),
        gsend=dma((bits, heads, plane)),
        grecv=dma((heads, plane)),
        psend=dma((bits, plane, 2)),
        precv=dma((bits, plane, 2)),
        csend=dma((heads,)),
        crecv=dma((heads,)),
        ysend=dma((2,)),
        yrecv=dma((2,)),
    )


def y_sum(place, r, slot, partial, meanwhile=None):
    r.ys[slot] = partial.astype(BF16)
    copy = remote(r.ys.at[slot], r.yr.at[slot], r.ysend.at[slot], r.yrecv.at[slot], place.y_peer())
    copy.start()
    if meanwhile is not None:
        meanwhile()
    copy.wait()
    return r.ys[slot].astype(F32) + r.yr[slot].astype(F32)


def forward_kernel(cfg, layer, names, *refs):
    inputs, refs = refs[:IN_COUNT], refs[IN_COUNT:]
    streams, params = Streams(*inputs[:3]), Params(*inputs[3:])
    out, scratch = Kept(*refs[: len(Kept._fields)]), refs[len(Kept._fields) :]
    r = gathered(out, streams, params, **dict(zip(names, scratch, strict=True)))
    r.second, r.renewed = streams.second, out.second
    place = Place(cfg)
    tok, heads = cfg.tok, cfg.heads
    band = heads * tok
    one = slice(layer, layer + 1)
    loads = [
        pltpu.make_async_copy(src.at[layer], dst, r.wsem.at[i])
        for i, (src, dst) in enumerate(
            (
                (r.wq_hbm, r.wq),
                (r.wv_hbm, r.wv),
                (r.wm_hbm, r.wm),
                (r.we_hbm, r.we),
                (r.ws_hbm, r.ws),
            )
        )
    ]
    for load in loads:
        load.start()
    normed = norm_parts(r.second[...])[0] * r.attention_gain[one, :] + r.attention_shift[one, :]
    normed = normed.astype(BF16)
    loads[0].wait()
    loads[1].wait()
    queries = dot(normed, r.wq[...]).astype(BF16)
    values = dot(normed, r.wv[...]).astype(BF16)
    for head in range(heads):
        r.zs[head, :, :DH] = queries[:, head * DH : (head + 1) * DH]
        r.zs[head, :, DH:] = values[:, head * DH : (head + 1) * DH]

    def block(head, spot):
        return r.tokens.at[pl.ds(pl.multiple_of((spot * heads + head) * tok, tok), tok), :]

    place.greet()
    sent = z_exchange(
        cfg,
        place,
        lambda head: r.zs.at[head],
        lambda head: block(head, place.member),
        r.zsend,
        r.zrecv,
    )
    block(place.head, place.member)[...] = r.zs[place.head]
    rank_rows(cfg, r.buckets[layer, place.round, pl.ds(place.head, 1), :], r.rank)

    spread = Doubling(
        place, [place.z_source(step) for step in range(heads)], block, r.gsend, r.grecv
    )
    for step in range(heads):
        if step > 0:
            z_arrival(place, block(place.z_source(step), place.member), r.zrecv, step).wait_recv()
        spread.offer(place.z_source(step))
    spread.receive()
    base = place.part * cfg.rows

    def store_rows(c, found):
        r.sorted[pl.ds(pl.multiple_of(CHUNK + c * 512, CHUNK), 512), :] = found.astype(BF16)

    def store_halo(c, found):
        r.sorted[0:CHUNK, :] = found.astype(BF16)

    sort_rows(cfg, r.rank, r.tokens, store_rows, base, 512, cfg.rows // 512)
    if cfg.parts == 1:
        r.sorted[0:CHUNK, :] = r.sorted[cfg.rows : cfg.ext, :]
    else:
        sort_rows(cfg, r.rank, r.tokens, store_halo, base + cfg.total - CHUNK, CHUNK, 1)
    raw = r.sorted[:, :DH].astype(F32)
    r.keys[...] = (raw * key_scale(raw)).astype(BF16)
    mask = window_mask()
    lane = lax.broadcasted_iota(jnp.int32, (CHUNK, LANES), 1)

    def attend(c, _):
        at = pl.multiple_of(c * CHUNK, CHUNK)
        query = r.sorted[pl.ds(at + CHUNK, CHUNK), :DH]
        scores = dot_nt(query, r.keys[pl.ds(at, 2 * CHUNK), :]) / math.sqrt(DH)
        scores = jnp.where(mask, scores, -1000000000.0)
        peak = jnp.max(scores, axis=-1, keepdims=True)
        powers = jnp.exp(scores - peak)
        summed = jnp.sum(powers, axis=-1, keepdims=True)
        weights = (powers / summed).astype(BF16)
        output = dot(weights, r.sorted[pl.ds(at, 2 * CHUNK), DH:])
        high, middle, low = split_three(peak + jnp.log(summed))
        extra = jnp.where(lane == 0, high, 0.0)
        extra = jnp.where(lane == 1, middle, extra)
        extra = jnp.where(lane == 2, low, extra)
        extra = jnp.where(lane == 3, 1.0, extra)
        r.attended[pl.ds(at, CHUNK), :DH] = output.astype(BF16)
        r.attended[pl.ds(at, CHUNK), DH:2 * DH] = extra.astype(BF16)
        r.attended[pl.ds(at, CHUNK), 2 * DH :] = (output - output.astype(BF16).astype(F32)).astype(BF16)
        return 0

    lax.fori_loop(0, cfg.rows // CHUNK, attend, 0)

    def unsort(spot):
        found = dot(unsort_pick(cfg, r.rank, spot, base, cfg.rows), r.attended[...])
        r.part[spot] = found[:, :DH] + found[:, 2 * DH :]
        extra = jnp.transpose(found[:, DH:2 * DH])
        row = extra[0:1] + extra[1:2] + extra[2:3] + (1.0 - extra[3:4]) * AWAY
        r.lrow[spot] = jnp.broadcast_to(row, (8, band))

    def pass_part(k, spot):
        peer = place.bit_peer(k)
        return [
            remote(mine.at[spot], theirs.at[k, spot], r.psend.at[k, spot, i], r.precv.at[k, spot, i], peer)
            for i, (mine, theirs) in enumerate(((r.part, r.part_in), (r.lrow, r.lrow_in)))
        ]

    def first_half(i, _):
        unsort(place.given(0, i))
        for copy in pass_part(0, place.given(0, i)):
            copy.start()
        return 0

    def second_half(i, _):
        unsort(place.kept(0, i))
        return 0

    lax.fori_loop(0, place.group(0), first_half, 0)
    lax.fori_loop(0, place.group(0), second_half, 0)

    def merge(k, spot):
        for copy in pass_part(k, spot):
            copy.wait_recv()
        mine = rows_to_columns(r.lrow[spot][0:1])
        other = rows_to_columns(r.lrow_in[k, spot][0:1])
        highest = jnp.maximum(mine, other)
        share = jnp.exp(mine - highest)
        share_in = jnp.exp(other - highest)
        both = share + share_in
        merged = (r.part[spot].astype(F32) * share + r.part_in[k, spot].astype(F32) * share_in) / both
        return merged, jnp.transpose(highest + jnp.log(both))[0:8]

    for k in range(cfg.bits - 1):
        for giving in (True, False):
            for i in range(place.group(k + 1)):
                spot = place.given(k + 1, i) if giving else place.kept(k + 1, i)
                merged, joint = merge(k, spot)
                r.part[spot] = merged
                r.lrow[spot] = joint
                if giving:
                    for copy in pass_part(k + 1, spot):
                        copy.start()
    merged, joint = merge(cfg.bits - 1, place.member)
    r.comb[...] = merged
    r.joint[...] = joint
    for head in range(heads):
        r.low_out[head] = merged[head * tok : (head + 1) * tok].astype(BF16)
    back = z_exchange(
        cfg, place, lambda head: r.low_out.at[head], lambda head: r.low_in.at[head], r.csend, r.crecv
    )
    r.low_in[place.head] = r.low_out[place.head]
    loads[2].wait()
    for step in range(1, heads):
        z_arrival(place, r.low_in.at[place.z_source(step)], r.crecv, step).wait_recv()
    low = jnp.concatenate([r.low_in[head] for head in range(heads)], axis=1)

    def finish_sends():
        spread.finish()
        for copy in sent + back:
            copy.wait_send()
        for k in range(cfg.bits):
            for i in range(place.group(k)):
                for copy in pass_part(k, place.given(k, i)):
                    copy.wait_send()
        r.normed_t[...] = jnp.transpose(normed)
        r.low_t[...] = jnp.transpose(low)

    mixed = (
        r.first[...]
        + y_sum(place, r, 0, dot(low, r.wm[...]), finish_sends)
        + r.mix_bias[one, :]
    )
    r.mixed[...] = mixed
    normed_two = norm_parts(mixed)[0] * r.forward_gain[one, :] + r.forward_shift[one, :]
    normed_two = normed_two.astype(BF16)
    loads[3].wait()
    hidden = dot(normed_two, r.we[...]) + r.expand_bias[one, :]
    r.hidden[...] = hidden
    active = (hidden * (1.0 + lax.erf(hidden * math.sqrt(0.5))) * 0.5).astype(BF16)
    loads[4].wait()

    def turn():
        r.normed_two_t[...] = jnp.transpose(normed_two)
        r.active_t[...] = jnp.transpose(active)

    r.renewed[...] = (
        r.second[...] + y_sum(place, r, 1, dot(active, r.ws[...]), turn) + r.shrink_bias[one, :]
    )


def unsort_pick(cfg, rank_ref, spot, base, rows):
    band = cfg.heads * cfg.tok
    ranks = rank_ref[0:1, pl.ds(pl.multiple_of(spot * band, band), band)]
    ranks = rows_to_columns(ranks.astype(F32)).astype(jnp.int32)[:, 0:1]
    places = base + lax.broadcasted_iota(jnp.int32, (band, rows), 1)
    if cfg.parts > 1:
        places = places % cfg.total
    return (ranks == places).astype(BF16)


IN_COUNT = len(Streams._fields) + len(Params._fields)


def forward_call(cfg, layer, streams, params):
    scratch = forward_scratch(cfg)
    whole = pl.BlockSpec(memory_space=pltpu.VMEM)
    apart = pl.BlockSpec(memory_space=pl.ANY)
    specs = Params(*[whole] * len(params))._replace(
        wq_hbm=apart, wv_hbm=apart, wm_hbm=apart, we_hbm=apart, ws_hbm=apart
    )
    outs = pl.pallas_call(
        functools.partial(forward_kernel, cfg, layer, list(scratch)),
        out_shape=[jax.ShapeDtypeStruct(*shape) for shape in saved_shapes(cfg)],
        in_specs=[whole] * len(streams) + list(specs),
        out_specs=[whole] * len(Kept._fields),
        scratch_shapes=list(scratch.values()),
        compiler_params=pltpu.CompilerParams(
            collective_id=layer, has_side_effects=True, vmem_limit_bytes=VMEM_LIMIT
        ),
        name=f"forward_{layer}",
    )(*streams, *params)
    return Kept(*outs)


RING = 4


def saved_shapes(cfg):
    tok, feats, band = cfg.tok, cfg.feats, cfg.heads * cfg.tok
    return Kept(
        second=((tok, feats), F32),
        mixed=((tok, feats), F32),
        sorted=((cfg.ext, 2 * DH), BF16),
        comb=((band, DH), F32),
        joint=((8, band), F32),
        hidden=((tok, cfg.hid), F32),
        rank=((8, cfg.total), jnp.int32),
        normed_t=((feats, tok), BF16),
        normed_two_t=((feats, tok), BF16),
        active_t=((cfg.hid, tok), BF16),
        low_t=((cfg.width, tok), BF16),
    )


def backward_scratch(cfg):
    tok, heads, plane, bits = cfg.tok, cfg.heads, cfg.plane, cfg.bits
    band = heads * tok
    dma = pltpu.SemaphoreType.DMA
    share = cfg.feats // cfg.seq
    return dict(
        wq=pltpu.VMEM((cfg.feats, cfg.width), BF16),
        wv=pltpu.VMEM((cfg.feats, cfg.width), BF16),
        wm=pltpu.VMEM((cfg.width, cfg.feats), BF16),
        we=pltpu.VMEM((cfg.feats, cfg.hid), BF16),
        ws=pltpu.VMEM((cfg.hid, cfg.feats), BF16),
        gs=pltpu.VMEM((heads, tok, DH), BF16),
        gtokens=pltpu.VMEM((cfg.total, 2 * DH), BF16),
        arow=pltpu.VMEM((LAYERS, plane, 8, band), F32),
        gsorted=pltpu.VMEM((cfg.rows, DH), BF16),
        stats=pltpu.VMEM((cfg.rows, LANES), F32),
        keys=pltpu.VMEM((cfg.ext, DH), BF16),
        dq=pltpu.VMEM((cfg.ext, DH), F32),
        dk=pltpu.VMEM((cfg.ext, DH), F32),
        dv=pltpu.VMEM((cfg.ext, DH), F32),
        grads=pltpu.VMEM((cfg.ext, 2 * DH), BF16),
        part=pltpu.VMEM((plane, band, 2 * DH), BF16),
        part_in=pltpu.VMEM((plane, band, 2 * DH), BF16),
        home_out=pltpu.VMEM((heads, tok, 2 * DH), BF16),
        home_in=pltpu.VMEM((heads, tok, 2 * DH), BF16),
        ys=pltpu.VMEM((2, tok, cfg.feats), BF16),
        yr=pltpu.VMEM((2, tok, cfg.feats), BF16),
        vectors=pltpu.VMEM((8, cfg.feats), F32),
        ubuf=pltpu.VMEM((RING, plane, heads, share, 512), BF16),
        uin=pltpu.VMEM((RING, plane, heads, share, 512), BF16),
        uz=pltpu.VMEM((RING, heads, share, 512), BF16),
        vbuf=pltpu.VMEM((LAYERS, plane, heads, 8, LANES), F32),
        vin=pltpu.VMEM((LAYERS, plane, heads, 8, LANES), F32),
        vz=pltpu.VMEM((LAYERS, heads, 8, LANES), F32),
        wsem=dma((5,)),
        lsem=dma((LAYERS, len(Kept._fields))),
        zsend=dma((LAYERS, heads)),
        zrecv=dma((LAYERS, heads)),
        gsend=dma((LAYERS, bits, heads, plane)),
        grecv=dma((LAYERS, heads, plane)),
        asend=dma((LAYERS, bits, 1, plane)),
        arecv=dma((LAYERS, 1, plane)),
        psend=dma((LAYERS, bits, plane)),
        precv=dma((LAYERS, bits, plane)),
        csend=dma((LAYERS, heads)),
        crecv=dma((LAYERS, heads)),
        ysend=dma((2,)),
        yrecv=dma((2,)),
        usend=dma((RING, bits + heads)),
        urecv=dma((RING, bits + heads)),
        vsend=dma((LAYERS, bits + heads)),
        vrecv=dma((LAYERS, bits + heads)),
    )


class Unit:
    def __init__(self, place, fill, done, buf, arrive, zbuf, send, recv):
        self.place, self.fill, self.done = place, fill, done
        self.buf, self.arrive, self.zbuf, self.send, self.recv = buf, arrive, zbuf, send, recv
        self.stage = 0

    def halved(self, k):
        place, plane = self.place, self.place.cfg.plane
        group = place.group(k)
        start = plane - plane // 2**k
        shape = (group, 2 ** (k + 1)) + self.buf.shape[1:]
        spot = (1 - place.bit(k)) * 2**k + place.member % 2**k
        return remote(
            self.buf.reshape(*shape).at[:, spot],
            self.arrive.at[start : start + group],
            self.send.at[k],
            self.recv.at[k],
            place.bit_peer(k),
        )

    def across(self, step):
        place = self.place
        head, peer = place.z_peer(step)
        at = place.cfg.bits + step
        return remote(
            self.buf.at[place.member, head], self.zbuf.at[step], self.send.at[at], self.recv.at[at], peer
        )

    def advance(self):
        place, cfg = self.place, self.place.cfg
        k = self.stage - 1
        if self.stage == 0:
            self.fill(self.buf)
        elif k < cfg.bits:
            self.halved(k).wait_recv()
            start = cfg.plane - cfg.plane // 2**k
            for i in range(place.group(k)):
                spot = place.kept(k, i)
                both = self.buf[spot].astype(F32) + self.arrive[start + i].astype(F32)
                self.buf[spot] = both.astype(self.buf.dtype)
        else:
            total = self.buf[place.member, place.head].astype(F32)
            for step in range(1, cfg.heads):
                self.across(step).wait_recv()
                total = total + self.zbuf[step].astype(F32)
            self.done(total)
            for k in range(cfg.bits):
                self.halved(k).wait_send()
            for step in range(1, cfg.heads):
                self.across(step).wait_send()
        self.stage += 1
        if self.stage <= cfg.bits:
            self.halved(self.stage - 1).start()
        elif self.stage == cfg.bits + 1:
            for step in range(1, cfg.heads):
                self.across(step).start()
        return self.stage <= cfg.bits + 1


class Pump:
    def __init__(self):
        self.waiting, self.flying = [], []

    def tick(self, times=1):
        for _ in range(times):
            self.flying = [unit for unit in self.flying if unit.advance()]
            if self.waiting:
                unit = self.waiting.pop(0)()
                unit.advance()
                self.flying.append(unit)

    def drain(self):
        while self.waiting or self.flying:
            self.tick()


def backward_kernel(cfg, names, *refs):
    params, refs = Params(*refs[: len(Params._fields)]), refs[len(Params._fields) :]
    (first_cot, second_cot), refs = refs[:2], refs[2:]
    held = []
    for _ in range(2 * LAYERS):
        held.append(Kept(*refs[: len(Kept._fields)]))
        refs = refs[len(Kept._fields) :]
        if len(held) == LAYERS:
            out, refs = Grads(*refs[: len(Grads._fields)]), refs[len(Grads._fields) :]
    stored, held = held[:LAYERS], held[LAYERS:]
    r = gathered(params, out, **dict(zip(names, refs, strict=True)))
    place = Place(cfg)
    tok, heads, plane, width = cfg.tok, cfg.heads, cfg.plane, cfg.width
    band = heads * tok
    share = cfg.feats // cfg.seq
    base = place.part * cfg.rows
    pump = Pump()
    count = [0]

    def weight_load(i, layer):
        source = (r.ws_hbm, r.we_hbm, r.wm_hbm, r.wq_hbm, r.wv_hbm)[i]
        target = (r.ws, r.we, r.wm, r.wq, r.wv)[i]
        return pltpu.make_async_copy(source.at[layer], target, r.wsem.at[i])

    def saved_load(layer, ref):
        i = [ref is other for other in held[layer]].index(True)
        return pltpu.make_async_copy(stored[layer][i], ref, r.lsem.at[layer, i])

    def queue(fill, done):
        def make():
            slot = count[0] % RING
            count[0] += 1
            return Unit(
                place, fill, done, r.ubuf.at[slot], r.uin.at[slot], r.uz.at[slot], r.usend.at[slot], r.urecv.at[slot]
            )

        pump.waiting.append(make)

    def product(lines, right):
        def fill(buf):
            for head in range(heads):
                found = dot(lines(head), right)
                buf[:, head] = found.reshape(plane, share, 512).astype(BF16)

        return fill

    def queue_expand(layer, hidden_grad):
        lhs = held[layer].normed_two_t
        for j in range(cfg.hid // 512):

            def done(total, j=j):
                r.out_we[layer, :, j * 512 : (j + 1) * 512] = total

            queue(
                product(
                    lambda head: lhs[head * plane * share : (head + 1) * plane * share, :],
                    hidden_grad[:, j * 512 : (j + 1) * 512],
                ),
                done,
            )

    def queue_shrink(layer, branch):
        lhs = held[layer].active_t
        deep = cfg.hid // cfg.seq
        for h in range(deep // share):
            for j in range(cfg.feats // 512):

                def lines(head, h=h):
                    rows = lhs[head * plane * deep : (head + 1) * plane * deep, :]
                    rows = rows.reshape(plane, deep, tok)[:, h * share : (h + 1) * share]
                    return rows.reshape(plane * share, tok)

                def done(total, h=h, j=j):
                    r.out_ws[layer, h * share : (h + 1) * share, j * 512 : (j + 1) * 512] = total

                queue(product(lines, branch[:, j * 512 : (j + 1) * 512]), done)

    def queue_mixing(layer, mix_low):
        lhs = held[layer].low_t
        deep = width // cfg.seq
        folds = share // deep

        def fill(buf):
            for head in range(heads):
                rows = lhs[head * plane * deep : (head + 1) * plane * deep, :]
                pieces = [
                    dot(rows, mix_low[:, j * 512 : (j + 1) * 512]).reshape(plane, deep, 512)
                    for j in range(folds)
                ]
                buf[:, head] = jnp.concatenate(pieces, axis=1).astype(BF16)

        def done(total):
            for j in range(folds):
                r.out_wm[layer, :, j * 512 : (j + 1) * 512] = total[j * deep : (j + 1) * deep]

        queue(fill, done)

    def queue_attention(layer, grad, out):
        lhs = held[layer].normed_t

        def done(total):
            out[layer] = total

        queue(product(lambda head: lhs[head * plane * share : (head + 1) * plane * share, :], grad), done)

    def queue_vectors(layer):
        def fill(buf):
            deep = cfg.hid // cfg.seq
            for p in range(cfg.seq):
                at = p * share // LANES * LANES
                tile = r.vectors[:, at : at + LANES]
                at = p * deep // LANES * LANES
                line, at = 6 + at // cfg.feats, at % cfg.feats
                extra = r.vectors[line : line + 1, at : at + LANES]
                buf[p % plane, p // plane, 0:6] = tile[0:6]
                buf[p % plane, p // plane, 6:8] = jnp.broadcast_to(extra, (2, LANES))

        def done(total):
            r.out_small[layer] = total

        def make():
            return Unit(
                place, fill, done, r.vbuf.at[layer], r.vin.at[layer], r.vz.at[layer], r.vsend.at[layer], r.vrecv.at[layer]
            )

        pump.waiting.append(make)

    order = list(reversed(range(LAYERS)))
    for i in range(5):
        weight_load(i, order[0]).start()
    for layer in order:
        k = held[layer]
        for ref in (k.active_t, k.hidden, k.mixed, k.normed_two_t, k.comb, k.joint, k.sorted):
            saved_load(layer, ref).start()
        for ref in (k.rank, k.low_t, k.second, k.normed_t):
            saved_load(layer, ref).start()
    place.greet()

    for layer in order:
        one = slice(layer, layer + 1)
        after = layer - 1

        saved = held[layer]

        def arrived(*fields):
            for field in fields:
                saved_load(layer, field).wait()

        def next_weight(*numbers):
            if after >= 0:
                for i in numbers:
                    weight_load(i, after).start()

        second_grad = second_cot if layer == order[0] else r.second_out
        first_grad = first_cot if layer == order[0] else r.first_out
        branch = second_grad[...].astype(BF16)
        arrived(saved.active_t, saved.hidden)
        queue_shrink(layer, branch)
        pump.tick()
        r.vectors[0:1, :] = jnp.sum(branch.astype(F32), axis=0, keepdims=True)
        hidden = saved.hidden[...]
        slope = 0.5 * (1.0 + lax.erf(hidden * math.sqrt(0.5)))
        slope = slope + hidden * jnp.exp(-0.5 * hidden * hidden) * (1.0 / math.sqrt(2.0 * math.pi))
        weight_load(0, layer).wait()
        hidden_grad = (dot_nt(branch, r.ws[...]) * slope).astype(BF16)
        next_weight(0)
        weight_load(1, layer).wait()
        partial = dot_nt(hidden_grad, r.we[...])
        next_weight(1)
        arrived(saved.mixed, saved.normed_two_t)

        def during_two():
            summed = jnp.sum(hidden_grad.astype(F32), axis=0, keepdims=True)
            for i in range(cfg.hid // cfg.feats):
                r.vectors[6 + i : 7 + i, :] = summed[:, i * cfg.feats : (i + 1) * cfg.feats]
            queue_expand(layer, hidden_grad)
            pump.tick(2)

        two_grad = y_sum(place, r, 0, partial, during_two)
        xhat, scale = norm_parts(saved.mixed[...])
        mixed_grad = first_grad[...] + norm_back(xhat, scale, r.forward_gain[one, :], two_grad)
        r.first_out[...] = mixed_grad
        mix_low = mixed_grad.astype(BF16)
        weight_load(2, layer).wait()
        combined_grad = dot_nt(mix_low, r.wm[...]).astype(BF16)
        next_weight(2)
        for head in range(heads):
            r.gs[head] = combined_grad[:, head * DH : (head + 1) * DH]

        def rows_of(spot, head):
            return pl.ds(pl.multiple_of((spot * heads + head) * tok, tok), tok)

        def block(head, spot):
            return r.gtokens.at[rows_of(spot, head), :DH]

        sent = z_exchange(
            cfg,
            place,
            lambda head: r.gs.at[head],
            lambda head: block(head, place.member),
            r.zsend.at[layer],
            r.zrecv.at[layer],
        )
        block(place.head, place.member)[...] = r.gs[place.head]
        r.vectors[1:2, :] = jnp.sum(mix_low.astype(F32), axis=0, keepdims=True)
        r.vectors[2:3, :] = jnp.sum(two_grad * xhat, axis=0, keepdims=True)
        r.vectors[3:4, :] = jnp.sum(two_grad, axis=0, keepdims=True)
        arrived(saved.sorted, saved.rank, saved.comb, saved.joint, saved.low_t)
        rank = saved.rank
        rows = saved.sorted
        queue_mixing(layer, mix_low)
        raw = rows[:, :DH].astype(F32)
        r.keys[...] = (raw * key_scale(raw)).astype(BF16)
        pump.tick()
        spread = Doubling(
            place,
            [place.z_source(step) for step in range(heads)],
            block,
            r.gsend.at[layer],
            r.grecv.at[layer],
        )
        for step in range(heads):
            if step > 0:
                spot = block(place.z_source(step), place.member)
                z_arrival(place, spot, r.zrecv.at[layer], step).wait_recv()
            spread.offer(place.z_source(step))
        mine = r.gtokens[pl.ds(pl.multiple_of(place.member * band, band), band), :DH].astype(F32)
        inner = jnp.sum(jnp.transpose(mine * saved.comb[...]), axis=0, keepdims=True)
        line = lax.broadcasted_iota(jnp.int32, (8, band), 0)
        r.arow[layer, place.member] = jnp.where(
            line == 0, saved.joint[...], jnp.broadcast_to(inner, (8, band))
        )
        extras = Doubling(
            place,
            [0],
            lambda key, spot: r.arow.at[layer, spot],
            r.asend.at[layer],
            r.arecv.at[layer],
        )
        extras.offer(0)
        spread.receive()
        extras.receive()
        pump.tick()
        lines = lax.broadcasted_iota(jnp.int32, (LANES, band), 0)
        for spot in range(plane):
            pieces = split_three(r.arow[layer, spot][0:1]) + split_three(r.arow[layer, spot][1:2])
            table = jnp.zeros((LANES, band), F32)
            for i, piece in enumerate(pieces):
                table = jnp.where(lines == i, piece, table)
            r.gtokens[spot * band : (spot + 1) * band, DH:] = jnp.transpose(table).astype(BF16)

        def store_rows(c, found):
            at = pl.ds(pl.multiple_of(c * 512, 512), 512)
            r.gsorted[at, :] = found[:, :DH].astype(BF16)
            r.stats[at, :] = found[:, DH:]

        sort_rows(cfg, rank, r.gtokens, store_rows, base, 512, cfg.rows // 512)
        pump.tick()
        r.dk[...] = jnp.zeros((cfg.ext, DH), F32)
        r.dv[...] = jnp.zeros((cfg.ext, DH), F32)
        r.dq[0:CHUNK, :] = jnp.zeros((CHUNK, DH), F32)
        mask = window_mask()

        def attend(c, _):
            at = pl.multiple_of(c * CHUNK, CHUNK)
            own = pl.ds(at + CHUNK, CHUNK)
            window = pl.ds(at, 2 * CHUNK)
            query = rows[own, :DH]
            near = r.keys[window, :]
            grad = r.gsorted[pl.ds(at, CHUNK), :]
            stats = r.stats[pl.ds(at, CHUNK), :]
            joint = stats[:, 0:1] + stats[:, 1:2] + stats[:, 2:3]
            inner = stats[:, 3:4] + stats[:, 4:5] + stats[:, 5:6]
            scores = dot_nt(query, near) / math.sqrt(DH)
            scores = jnp.where(mask, scores, -1000000000.0)
            probs = jnp.exp(scores - joint)
            prob_grad = dot_nt(grad, rows[window, DH:])
            score_grad = (probs * (prob_grad - inner) / math.sqrt(DH)).astype(BF16)
            r.dq[own, :] = dot(score_grad, near)
            r.dk[window, :] = r.dk[window, :] + dot_tn(score_grad, query)
            r.dv[window, :] = r.dv[window, :] + dot_tn(probs.astype(BF16), grad)
            return 0

        half = cfg.rows // CHUNK // 2
        lax.fori_loop(0, half, attend, 0)
        pump.tick()
        lax.fori_loop(half, cfg.rows // CHUNK, attend, 0)
        if cfg.parts == 1:
            last = slice(cfg.rows, cfg.ext)
            r.dk[last, :] = r.dk[last, :] + r.dk[0:CHUNK, :]
            r.dv[last, :] = r.dv[last, :] + r.dv[0:CHUNK, :]
        raw = rows[:, :DH].astype(F32)
        scale = key_scale(raw)
        dk = r.dk[...]
        inner = jnp.mean(raw * dk, axis=-1, keepdims=True)
        r.grads[:, :DH] = (
            r.dq[...] + scale * dk - raw * (scale * scale * scale * inner)
        ).astype(BF16)
        r.grads[:, DH:] = r.dv[...].astype(BF16)
        pump.tick()
        skip = CHUNK if cfg.parts == 1 else 0

        def unsort(spot):
            start = base if cfg.parts == 1 else base + cfg.total - CHUNK
            pick = unsort_pick(cfg, rank, spot, start, cfg.ext - skip)
            r.part[spot] = dot(pick, r.grads[skip:, :]).astype(BF16)

        def pass_part(k, spot):
            return remote(
                r.part.at[spot],
                r.part_in.at[plane - plane // 2**k + spot // 2 ** (k + 1)],
                r.psend.at[layer, k, spot],
                r.precv.at[layer, k, spot // 2 ** (k + 1)],
                place.bit_peer(k),
            )

        def first_half(i, _):
            unsort(place.given(0, i))
            pass_part(0, place.given(0, i)).start()
            return 0

        def second_half(i, _):
            unsort(place.kept(0, i))
            return 0

        lax.fori_loop(0, place.group(0), first_half, 0)
        lax.fori_loop(0, place.group(0), second_half, 0)

        def merge(k, spot):
            pass_part(k, spot).wait_recv()
            other = r.part_in[plane - plane // 2**k + spot // 2 ** (k + 1)]
            return (r.part[spot].astype(F32) + other.astype(F32)).astype(BF16)

        for k in range(cfg.bits - 1):
            for giving in (True, False):
                for i in range(place.group(k + 1)):
                    spot = place.given(k + 1, i) if giving else place.kept(k + 1, i)
                    r.part[spot] = merge(k, spot)
                    if giving:
                        pass_part(k + 1, spot).start()
        pump.tick()
        merged = merge(cfg.bits - 1, place.member)
        for head in range(heads):
            r.home_out[head] = merged[head * tok : (head + 1) * tok]
        back = z_exchange(
            cfg,
            place,
            lambda head: r.home_out.at[head],
            lambda head: r.home_in.at[head],
            r.csend.at[layer],
            r.crecv.at[layer],
        )
        r.home_in[place.head] = r.home_out[place.head]
        arrived(saved.second, saved.normed_t)
        weight_load(3, layer).wait()
        weight_load(4, layer).wait()
        pump.tick()
        for step in range(1, heads):
            spot = r.home_in.at[place.z_source(step)]
            z_arrival(place, spot, r.crecv.at[layer], step).wait_recv()
        query_grad = jnp.concatenate([r.home_in[head][:, :DH] for head in range(heads)], axis=1)
        value_grad = jnp.concatenate([r.home_in[head][:, DH:] for head in range(heads)], axis=1)
        one_grad = dot_nt(query_grad, r.wq[...]) + dot_nt(value_grad, r.wv[...])
        next_weight(3, 4)

        def during_one():
            queue_attention(layer, query_grad, r.out_wq)
            queue_attention(layer, value_grad, r.out_wv)
            spread.finish()
            extras.finish()
            for copy in sent + back:
                copy.wait_send()
            for k in range(cfg.bits):
                for i in range(place.group(k)):
                    pass_part(k, place.given(k, i)).wait_send()
            pump.tick(2)

        one_grad = y_sum(place, r, 1, one_grad, during_one)
        xhat, scale = norm_parts(saved.second[...])
        dx = norm_back(xhat, scale, r.attention_gain[one, :], one_grad)
        r.second_out[...] = second_grad[...] + dx
        r.vectors[4:5, :] = jnp.sum(one_grad * xhat, axis=0, keepdims=True)
        r.vectors[5:6, :] = jnp.sum(one_grad, axis=0, keepdims=True)
        queue_vectors(layer)
        pump.waiting.insert(0, pump.waiting.pop())
        pump.tick()
    pump.drain()


def backward_call(cfg, params, cotangents, saved):
    scratch = backward_scratch(cfg)
    tok, feats = cfg.tok, cfg.feats
    share = feats // cfg.seq
    shapes = Grads(
        first_out=(tok, feats),
        second_out=(tok, feats),
        out_wq=(LAYERS, share, cfg.width),
        out_wv=(LAYERS, share, cfg.width),
        out_wm=(LAYERS, cfg.width // cfg.seq, feats),
        out_we=(LAYERS, share, cfg.hid),
        out_ws=(LAYERS, cfg.hid // cfg.seq, feats),
        out_small=(LAYERS, 8, LANES),
    )
    whole = pl.BlockSpec(memory_space=pltpu.VMEM)
    apart = pl.BlockSpec(memory_space=pl.ANY)
    specs = Params(*[apart] * len(params))._replace(attention_gain=whole, forward_gain=whole)
    held = [pltpu.VMEM(*shape) for shape in saved_shapes(cfg)] * LAYERS
    outs = pl.pallas_call(
        functools.partial(backward_kernel, cfg, list(scratch)),
        out_shape=[jax.ShapeDtypeStruct(shape, F32) for shape in shapes],
        in_specs=list(specs) + [whole] * 2 + [apart] * (LAYERS * len(Kept._fields)),
        out_specs=[whole] * len(shapes),
        scratch_shapes=held + list(scratch.values()),
        compiler_params=pltpu.CompilerParams(
            collective_id=LAYERS, has_side_effects=True, vmem_limit_bytes=VMEM_LIMIT
        ),
        name="backward",
    )(*params, *cotangents, *[array for kept in saved for array in kept])
    return Grads(*outs)


def shards(stream_one, stream_two, cotangent_one, cotangent_two, bucket_numbers, *params):
    cfg = sizes_of(lax.axis_size("seq"), stream_one, params[0], params[4])
    params = Params(*params)
    first, second = stream_one, stream_two
    saved = []
    for layer in range(LAYERS):
        kept = forward_call(cfg, layer, Streams(first, second, bucket_numbers), params)
        saved.append(kept._replace(second=second))
        first, second = kept.mixed, kept.second
    out = backward_call(cfg, params, (cotangent_one, cotangent_two), saved)
    index = lax.axis_index("seq")

    def columns(extent):
        share = extent // cfg.seq
        return lambda line: lax.dynamic_slice_in_dim(
            out.out_small[:, line], index * share % LANES, share, axis=1
        )

    small = columns(cfg.feats)
    return (
        first,
        second,
        out.first_out,
        out.second_out,
        out.out_wq,
        out.out_wv,
        out.out_wm,
        small(1),
        out.out_we,
        columns(cfg.hid)(6),
        out.out_ws,
        small(0),
        small(4),
        small(5),
        small(2),
        small(3),
    )


def solution(mesh):
    in_specs = (
        P("seq", None),
        P("seq", None),
        P("seq", None),
        P("seq", None),
        P(None, None, "mp", None),
        P(None, None, "mp"),
        P(None, None, "mp"),
        P(None, "mp", None),
        P(),
        P(None, None, "mp"),
        P(None, "mp"),
        P(None, "mp", None),
        P(),
        P(),
        P(),
        P(),
        P(),
    )
    out_specs = (
        P("seq", None),
        P("seq", None),
        P("seq", None),
        P("seq", None),
        P(None, "seq", "mp"),
        P(None, "seq", "mp"),
        P(None, ("mp", "seq"), None),
        P(None, "seq"),
        P(None, "seq", "mp"),
        P(None, ("mp", "seq")),
        P(None, ("mp", "seq"), None),
        P(None, "seq"),
        P(None, "seq"),
        P(None, "seq"),
        P(None, "seq"),
        P(None, "seq"),
    )
    return jax.shard_map(shards, mesh=mesh, in_specs=in_specs, out_specs=out_specs, check_vma=False)
```

time: 2930 us -> 365 us (0.12)
  waiting for transfers between devices: 1290 us -> 0 us
  local copies, waits for them, and re-layouts: 1250 us -> 10.7 us
  Pallas kernels: 0 us -> 349 us
  other arithmetic: 110 us -> 0 us
  blocking collectives: 98.5 us -> 0 us
  matrix products: 81 us -> 0 us
  starting transfers between devices: 70.7 us -> 0 us
    gather x44 -> x0, local copies, waits for them, and re-layouts: 1080 us -> none  [the longest x16 580 us: reorder(): return jnp.take_along_axis(values, row_order[..., None], axis=2)]
    reduce_scatter x5 -> x0, waiting for transfers between devices: 592 us -> none  [the longest x1 183 us: shards(): lax.psum_scatter(stacked[6], 'seq', scatter_dimension=1, tiled=True)]
    unnamed x26 -> x0, waiting for transfers between devices: 360 us -> none
    pallas_call x0 -> x3, Pallas kernels: none -> 349 us  [the longest x1 217 us: backward_call(): pl.pallas_call(functools.partial(backward_kernel, cfg, list(scratch)), ou...]
    psum x7 -> x0, waiting for transfers between devices: 218 us -> none  [the longest x4 134 us: model_sum(): return lax.psum(partial_sum, 'mp')]
    all_to_all x1 -> x0, blocking collectives: 98.5 us -> none  [layer_backward(): lax.all_to_all(padded_peers(rows_grad, sort_back, groups), 'seq', split_a...]
    sort x20 -> x0, local copies, waits for them, and re-layouts: 86.4 us -> none  [the longest x4 55.9 us: make_routing(): jnp.argsort(jnp.where(mine, 0, 1).astype(jnp.int32), axis=-1, stable=True)]
    all_to_all x11 -> x0, waiting for transfers between devices: 83.4 us -> none  [the longest x1 72 us: layer_backward(): lax.all_to_all(padded_peers(rows_grad, sort_back, groups), 'seq', split_a...]
  transfers between devices with their start and end apart: 34 -> 0, of which waited for: 28 -> 0; matrix products, arithmetic and copies ran while one was open for 16% -> 0% of each run, Pallas kernels for 0% -> 0%
where the time goes in v1:
time: 365 us; the launch traced here: 360 us
  Pallas kernels  349 us (96%)
  local copies, waits for them, and re-layouts  10.7 us (3%)
    pallas_call x1, Pallas kernels, backward_call(): pl.pallas_call(functools.partial(backward_kernel, cfg, list(scratch)), ou...  217 us
    pallas_call x2, Pallas kernels, forward_call(): pl.pallas_call(functools.partial(forward_kernel, cfg, layer, list(scratch...  132 us

profile of v1, /device:TPU:0, one launch (start us, length us, event | category | flops | bytes accessed | tf_op | source)
XLA Modules:
  0.0 360.5 jit_solution(3648139813073264952)
XLA Ops:
  0.6 67.3 %forward_0.1 = (f32[128,1024]{1,0:T(8,128)}, bf16[2176,256]{1,0:T(8,128)(2,1)}, f32[512,128]{1,0:T(8,128)}, f32[8,512]{1,0:T(8,128)}, f32[128,2048]{1,0:T(8,128)...) custom-call(f32[128,1024]{1,0:T(8,128)} %refs_0_.2, ...), custom_call_target="tpu_custom_call" | custom-call | tf_op jit(solution)/shard_map/forward_0/pallas_call | solution.py:576
  68.0 65.0 %forward_1.1 = (f32[128,1024]{1,0:T(8,128)}, bf16[2176,256]{1,0:T(8,128)(2,1)}, f32[512,128]{1,0:T(8,128)}, f32[8,512]{1,0:T(8,128)}, f32[128,2048]{1,0:T(8,128)...) custom-call(f32[128,1024]{1,0:T(8,128)} %get-tuple-element.46.refs_0, ...), custom_call_target="tpu_custom_call" | custom-call | tf_op jit(solution)/shard_map/forward_1/pallas_call | solution.py:576
  133.0 0.0 copy-start
  133.0 0.0 copy-start.3
  133.0 216.5 %backward.1 = (f32[128,1024]{1,0:T(8,128)}, f32[128,1024]{1,0:T(8,128)}, f32[2,64,512]{2,1,0:T(8,128)}, f32[2,64,512]{2,1,0:T(8,128)}, f32[2,32,1024]{2,1,0:T(8,...) custom-call(bf16[2,1024,512]{2,1,0:T(8,128)(2,1)} %refs_0_.3, ...), custom_call_target="tpu_custom_call" | custom-call | tf_op jit(solution)/shard_map/backward/pallas_call | solution.py:1148
  349.5 0.0 copy-start.5
  349.5 0.0 copy-start.4
  349.5 1.5 fusion
  351.1 0.6 constant_dynamic-slice_fusion
  351.7 0.6 constant_dynamic-slice_fusion.2
  352.3 0.6 constant_dynamic-slice_fusion.4
  353.0 0.0 copy-done
  353.0 0.8 copy.42
  353.8 0.8 copy.43
  354.6 0.0 copy-done.5
  354.6 0.8 copy.44
  355.4 0.0 copy-done.4
  355.4 0.8 copy.45
  356.2 0.7 copy.46
  356.9 0.7 copy.47
  357.6 0.0 copy-done.6
  357.6 0.7 copy.48
  358.3 1.0 copy.49
  359.3 1.0 copy.50
  (10 shorter events, 0.0 us)
Async XLA Ops:
  133.0 220.0 %copy-start = (f32[128,1024]{1,0:T(8,128)S(1)}, f32[128,1024]{1,0:T(8,128)}, u32[]{:S(2)}) copy-start(f32[128,1024]{1,0:T(8,128)} %get-tuple-element.105.refs_25_) | copy-start | bytes 1572868
  133.0 220.8 %copy-start.3 = (f32[128,1024]{1,0:T(8,128)S(1)}, f32[128,1024]{1,0:T(8,128)}, u32[]{:S(2)}) copy-start(f32[128,1024]{1,0:T(8,128)} %get-tuple-element.106) | copy-start | bytes 1572868
  349.5 5.1 %copy-start.5 = (f32[128,1024]{1,0:T(8,128)S(1)}, f32[128,1024]{1,0:T(8,128)}, u32[]{:S(2)}) copy-start(f32[128,1024]{1,0:T(8,128)} %get-tuple-element.107) | copy-start | bytes 1572868
  349.5 5.8 %copy-start.4 = (f32[128,1024]{1,0:T(8,128)S(1)}, f32[128,1024]{1,0:T(8,128)}, u32[]{:S(2)}) copy-start(f32[128,1024]{1,0:T(8,128)} %get-tuple-element.108) | copy-start | bytes 1572868
  353.0 3.2 copy-start.8
  353.8 3.1 copy-start.7
  353.8 3.8 %copy-start.6 = (f32[2,32,1024]{2,1,0:T(8,128)S(1)}, f32[2,32,1024]{2,1,0:T(8,128)}, u32[]{:S(2)}) copy-start(f32[2,32,1024]{2,1,0:T(8,128)} %get-tuple-element.111) | copy-start | bytes 786436
  354.6 3.7 %copy-start.2 = (f32[2,64,2048]{2,1,0:T(8,128)S(1)}, f32[2,64,2048]{2,1,0:T(8,128)}, u32[]{:S(2)}) copy-start(f32[2,64,2048]{2,1,0:T(8,128)} %get-tuple-element.113) | copy-start | bytes 3145732
  356.2 3.1 copy-start.1
